TPU v7x, 512 devices: a whole 4x8x8 slice. The times are simulated.
512 devices in a mesh: layer: 2 (over x_hi), gx: 32 (over z, x_lo, core), gy: 8 (over y).
Axes of the slice: x: 4 (x_hi: 2, x_lo: 2; x = x_hi * 2 + x_lo), y: 8, z: 8, core: 2. Of those that a mesh axis runs over, the one named last changes fastest.
Arguments:
- prev_vec: float32 [2, 64, 32, 32, 128], P('layer', 'gx', 'gy'), may hold values from -6 to 6
- cur_vec: float32 [2, 64, 32, 32, 128], P('layer', 'gx', 'gy'), may hold values from -6 to 6
- displace: float32 [2, 64, 32, 2, 128], P('layer', 'gx', 'gy'), may hold values from -0.15 to 0.15
- potential: float32 [2, 64, 32, 128], P('layer', 'gx', 'gy'), may hold values from -1.5 to 1.5
Outputs:
- first_term: float32 [2, 64, 32, 32, 128], P('layer', 'gx', 'gy')
- second_term: float32 [2, 64, 32, 32, 128], P('layer', 'gx', 'gy')
All inputs are finite; a program needn't handle non-finite values.
Results may differ from a plain program's by a relative error of at most 0.0003.
Values sent between devices are 32-bit elements; how exact they have to be, the bound alone decides.
A program may use at most 64 MiB of HBM per device.

v0:
```python
import math

import jax
import jax.numpy as jnp
import numpy as np
from jax import lax
from jax.experimental import pallas as pl
from jax.experimental.pallas import tpu as pltpu
from jax.sharding import PartitionSpec as P

MESH = pl.DeviceIdType.MESH
PATCH_X = 14
PATCH_Y = 4

v_pi = -2.7
v_sigma = 0.48
decay_len = 0.319
layer_gap = 3.35 / 1.42
cut_radius = 3.5
hop_scale = 12.0
twist_angle = 1.05 * math.pi / 180.0
root_three = math.sqrt(3.0)
cell_w = 4.0 * root_three
cell_h = 24.0
reach = 0.15

COLS = 8
RIM = 2
WIDE = COLS + 2 * RIM
STEPS = 5
ROWS = 32
AUX = 8
FULL = ROWS + AUX
atom_x = (0.0, root_three / 2.0, root_three / 2.0, 0.0)
atom_y = (0.0, 0.5, 1.5, 2.0)


def near_offsets():
    cos_t, sin_t = math.cos(twist_angle), math.sin(twist_angle)
    cells = []
    for s in range(4):
        col, row = np.meshgrid(np.arange(4 * PATCH_X), np.arange(8 * PATCH_Y), indexing="ij")
        x = (col - 2 * PATCH_X) * root_three + atom_x[s]
        y = (row - 4 * PATCH_Y) * 3.0 + atom_y[s]
        cells.append(np.stack([x.ravel(), y.ravel()], -1))
    places = np.concatenate(cells)
    turn = np.array([[cos_t - 1.0, -sin_t], [sin_t, cos_t - 1.0]])
    drift = places @ turn.T
    drift = np.concatenate([drift, -drift])
    slack = 2.0 * reach + 1e-3
    flat = math.sqrt(cut_radius**2 - layer_gap**2)
    plane, inter = [], []
    for step in range(-STEPS - 2, STEPS + 3):
        for col in range(-RIM - 2, RIM + 3):
            hit_plane = hit_inter = False
            for s in range(4):
                t = (s + step) % 4
                x = atom_x[s] - atom_x[t] - col * root_three
                y = atom_y[s] - atom_y[t] - 3.0 * ((s + step) // 4)
                hit_plane |= math.hypot(x, y) - slack * math.sqrt(2.0) < cut_radius
                gap = np.maximum(np.abs(np.array([x, y]) + drift) - slack, 0.0)
                hit_inter |= bool((np.hypot(gap[:, 0], gap[:, 1]) < flat).any())
            if hit_plane and (col, step) != (0, 0):
                plane.append((col, step))
            if hit_inter:
                inter.append((col, step))
    assert max(abs(c) for c, _ in plane + inter) <= RIM
    assert max(abs(s) for _, s in plane + inter) <= STEPS
    return plane, inter


PLANE, INTER = near_offsets()
TILE = (1, 0, 0)
SIDES = [(a, b, 0) for a in (0, 1) for b in (-1, 1)]
ENDS = [(a, b, c) for a in (0, 1) for b in (-1, 0, 1) for c in (-1, 1)]
PEERS = SIDES + [TILE] + ENDS


def peer(step):
    sizes = [lax.axis_size(a) for a in ("layer", "gx", "gy")]
    return tuple(
        lax.rem(lax.axis_index(a) + s + n, n) for a, s, n in zip(("layer", "gx", "gy"), step, sizes)
    )


def pick(index, table):
    value = jnp.full(index.shape, table[3], jnp.float32)
    for s in range(3):
        value = jnp.where(index == s, jnp.float32(table[s]), value)
    return value


def regroup(parts, lane):
    group = lane // 32
    results = []
    for a in range(4):
        value = parts[a]
        for b in range(4):
            if b != a:
                value = jnp.where(group == b, pltpu.roll(parts[b], (32 * (b - a)) % 128, 1), value)
        results.append(value)
    return results


def kernel(
    prev_hbm, cur_hbm, disp_hbm, pot_hbm, first_ref, second_ref,
    prev_in, cur_in, disp_in, pot_in, aux, prev_t, wide, wide2, end_out, end_in, end_out2, end_in2,
    rolled, spot, spot_rim, near_plane, near_inter, hop_plane, hop_inter,
    load_sem, send_sem, recv_sem,
):
    barrier = pltpu.get_barrier_semaphore()
    for step in PEERS:
        pl.semaphore_signal(barrier, inc=1, device_id=peer(step), device_id_type=MESH)
    loads = [
        pltpu.make_async_copy(src, dst, load_sem.at[i])
        for i, (src, dst) in enumerate(
            ((cur_hbm, cur_in), (disp_hbm, disp_in), (pot_hbm, pot_in), (prev_hbm, prev_in))
        )
    ]
    for load in loads:
        load.start()
    lane = lax.broadcasted_iota(jnp.int32, (8, 128), 1)
    zero = jnp.zeros((8, 128), jnp.float32)

    def to_columns(source, target, rows, first):
        for x in range(2):
            for g in range(rows // 8):
                parts = [source[0, x, y, 8 * g : 8 * g + 8, :] for y in range(4)]
                for i, value in enumerate(regroup(parts, lane)):
                    target[first + 4 * x + i, 8 * g : 8 * g + 8, :] = value

    loads[0].wait()
    to_columns(cur_in, wide.at[0], ROWS, RIM)
    loads[1].wait()
    loads[2].wait()
    for x in range(2):
        for y in range(4):
            aux[x, y] = zero
            aux[x, y, 0:2] = disp_in[0, x, y]
            aux[x, y, 2:3] = pot_in[0, x, y : y + 1]
        for i, value in enumerate(regroup([aux[x, y] for y in range(4)], lane)):
            wide[0, RIM + 4 * x + i, ROWS:FULL, :] = value

    def pack_ends(source, target, aux_too):
        for part in range(2 if aux_too else 1):
            count = 32 if part == 0 else COLS
            low, high = zero, zero
            for k in range(count):
                col, row = (k // 4, 8 * (k % 4)) if part == 0 else (k, ROWS)
                value = pltpu.roll(source[0, RIM + col, row : row + 8, :], (4 * k + 4) % 128, 1)
                low = jnp.where(lane // 4 == k, value, low)
                high = jnp.where(lane // 4 == (k + 1) % 32, value, high)
            target[0, 8 * part : 8 * part + 8, :] = low
            target[1, 8 * part : 8 * part + 8, :] = high

    pack_ends(wide, end_out, True)

    def exchange(phase, buffer, ends_from, ends_to):
        copies = []
        for n, step in enumerate(PEERS):
            layer, gx, gy = step
            if gy:
                source = ends_from.at[0 if gy > 0 else 1]
                target = ends_to.at[layer, 0 if gy > 0 else 1, 1 - gx]
            elif gx > 0:
                source, target = buffer.at[0, pl.ds(COLS, RIM)], buffer.at[layer, pl.ds(0, RIM)]
            elif gx < 0:
                source = buffer.at[0, pl.ds(RIM, RIM)]
                target = buffer.at[layer, pl.ds(RIM + COLS, RIM)]
            else:
                source, target = buffer.at[0, pl.ds(RIM, COLS)], buffer.at[1, pl.ds(RIM, COLS)]
            copy = pltpu.make_async_remote_copy(
                src_ref=source,
                dst_ref=target,
                send_sem=send_sem.at[phase, n],
                recv_sem=recv_sem.at[phase, n],
                device_id=peer(step),
                device_id_type=MESH,
            )
            copy.start()
            copies.append(copy)
        return copies

    pl.semaphore_wait(barrier, len(PEERS))
    copies = exchange(0, wide, end_out, end_in)
    loads[3].wait()
    to_columns(prev_in, prev_t, ROWS, 0)
    for copy in copies:
        copy.wait()

    def rim_of(col):
        side = jnp.where(col < RIM, 0, jnp.where(col < RIM + COLS, 1, 2))
        return side, lax.rem(col + COLS - RIM, COLS)

    def end_levels(low, high, k):
        picked = jnp.where(((lane + (124 - 4 * k)) & 127) < 64, high, low)
        return pltpu.roll(picked, 124 - 4 * k, 1)

    def shifted(value, rim, step):
        if step > 0:
            value = jnp.where(lane[: value.shape[0]] < step, rim, value)
        if step < 0:
            value = jnp.where(lane[: value.shape[0]] >= 128 + step, rim, value)
        return pltpu.roll(value, (-step) % 128, 1) if step else value

    def spot_step(t, carry):
        layer, col = t // WIDE, lax.rem(t, WIDE)
        side, own = rim_of(col)
        rim = end_levels(end_in[layer, 0, side, 8:16, :], end_in[layer, 1, side, 8:16, :], own)
        here = wide[layer, col, ROWS:FULL, :]
        for axis in range(2):
            spot[layer, axis, pl.ds(col, 1), :] = here[axis : axis + 1]
            spot_rim[layer, axis, pl.ds(col, 1), :] = rim[axis : axis + 1]
        return carry

    for layer in range(2):
        for axis in range(2):
            spot[layer, axis, 8:16, :] = zero
            spot_rim[layer, axis, 8:16, :] = zero
    lax.fori_loop(0, 2 * WIDE, spot_step, 0)

    layer_id = lax.axis_index("layer")
    cos_t, sin_t = math.cos(twist_angle), math.sin(twist_angle)
    upper = layer_id == 1
    cos_own = jnp.where(upper, jnp.float32(cos_t), jnp.float32(1.0))
    sin_own = jnp.where(upper, jnp.float32(sin_t), jnp.float32(0.0))

    row16 = lax.broadcasted_iota(jnp.int32, (16, 128), 0)
    lane16 = lax.broadcasted_iota(jnp.int32, (16, 128), 1)
    atom = lane16 & 3
    block = (lax.axis_index("gx") * 2 + (row16 + RIM) // 4 - 1 + 2 * lax.axis_size("gx")) % (
        2 * lax.axis_size("gx")
    )
    at_x = (
        ((row16 + RIM) & 3).astype(jnp.float32) * root_three
        + pick(atom, atom_x)
        - cell_w / 2.0
        + cell_w * ((block % PATCH_X).astype(jnp.float32) - (PATCH_X - 1) / 2.0)
    )
    at_y = (
        ((lane16 // 4) & 7).astype(jnp.float32) * 3.0
        + pick(atom, atom_y)
        - cell_h / 2.0
        + cell_h * ((lane16 // 32).astype(jnp.float32) - (PATCH_Y - 1) / 2.0)
    )
    turn_x = (cos_t - 1.0) * at_x - sin_t * at_y
    turn_y = sin_t * at_x + (cos_t - 1.0) * at_y
    own_on = jnp.where(upper, jnp.float32(1.0), jnp.float32(0.0))
    other_on = 1.0 - own_on

    def unturned(ref):
        return (
            cos_own * ref[0, 0] + sin_own * ref[0, 1],
            cos_own * ref[0, 1] - sin_own * ref[0, 0],
        )

    plane_here, plane_rim = unturned(spot), unturned(spot_rim)
    turns = (turn_x, turn_y)
    lane_all = lane16
    for axis in range(2):
        inter_here = spot[1, axis] + other_on * turns[axis]
        inter_rim = spot_rim[1, axis] + other_on * turns[axis]
        for step in range(-STEPS, STEPS + 1):
            for here, rim, target in (
                (plane_here[axis], plane_rim[axis], near_plane),
                (inter_here, inter_rim, near_inter),
            ):
                value = here
                if step > 0:
                    value = jnp.where(lane_all < step, rim, value)
                if step < 0:
                    value = jnp.where(lane_all >= 128 + step, rim, value)
                if step:
                    value = pltpu.roll(value, (-step) % 128, 1)
                target[axis, step + STEPS] = value
        spot[0, axis] = spot[0, axis] + own_on * turns[axis]

    inner = slice(RIM, RIM + COLS)
    own_plane = [near_plane[axis, STEPS, inner, :] for axis in range(2)]
    own_inter = [spot[0, axis, inner, :] for axis in range(2)]

    def atom_heights(index):
        return (index >> 2).astype(jnp.float32) * 3.0 + pick(index & 3, atom_y)

    log2e = 1.0 / math.log(2.0)
    inverse_cut = 1.0 / (cut_radius * cut_radius)
    scale = 2.0 / hop_scale
    sigma_part = v_sigma * math.exp((layer_gap - 1.0) / decay_len)

    def parts(own, near, col, step):
        base_x = pick(lane & 3, atom_x) - pick((lane + step + 8) & 3, atom_x)
        base_y = atom_heights(lane + 8) - atom_heights(lane + (step + 8))
        rows = slice(RIM + col, RIM + col + COLS)
        delta_x = (own[0] - near[0, step + STEPS, rows, :]) + (base_x - col * root_three)
        delta_y = (own[1] - near[1, step + STEPS, rows, :]) + base_y
        return delta_x * delta_x + delta_y * delta_y

    def envelope(dist_sq, inverse):
        spread = dist_sq * inverse
        fall = jnp.exp2(spread * (-log2e / decay_len) + log2e / decay_len)
        scaled = dist_sq * inverse_cut
        return fall * jnp.maximum(1.0 - scaled * scaled, 0.0)

    for n, (col, step) in enumerate(PLANE):
        dist_sq = parts(own_plane, near_plane, col, step)
        hop_plane[n] = envelope(dist_sq, lax.rsqrt(dist_sq)) * (v_pi * scale)
    for n, (col, step) in enumerate(INTER):
        dist_sq = parts(own_inter, near_inter, col, step) + layer_gap * layer_gap
        inverse = lax.rsqrt(dist_sq)
        cosine_sq = (inverse * inverse) * (layer_gap * layer_gap)
        mix = cosine_sq * ((sigma_part - v_pi) * scale) + v_pi * scale
        hop_inter[n] = envelope(dist_sq, inverse) * mix

    def shift_columns(buffer, ends):
        def step_of(t, carry):
            layer, col = t // WIDE, lax.rem(t, WIDE)
            side, own = rim_of(col)
            low, high = ends[layer, 0, side, 0:8, :], ends[layer, 1, side, 0:8, :]
            for g in range(4):
                rim = end_levels(low, high, own * 4 + g)
                here = buffer[layer, col, 8 * g : 8 * g + 8, :]
                for step in range(-STEPS, STEPS + 1):
                    rolled[layer, step + STEPS, col, 8 * g : 8 * g + 8, :] = shifted(here, rim, step)
            return carry

        lax.fori_loop(0, 2 * WIDE, step_of, 0)

    def apply(buffer, minus, minus_first, target, target_first):
        def column(col, carry):
            onsite = wide[0, col + RIM, ROWS + 2 : ROWS + 3, :] * scale
            total = [
                onsite * buffer[0, col + RIM, 8 * g : 8 * g + 8, :]
                - minus[col + minus_first, 8 * g : 8 * g + 8, :]
                for g in range(4)
            ]
            for layer, (offsets, hops) in enumerate(((PLANE, hop_plane), (INTER, hop_inter))):
                for n, (dcol, step) in enumerate(offsets):
                    weight = jnp.broadcast_to(hops[n, pl.ds(col, 1), :], (8, 128))
                    for g in range(4):
                        near = rolled[layer, step + STEPS, col + RIM + dcol, 8 * g : 8 * g + 8, :]
                        total[g] = total[g] + weight * near
            for g in range(4):
                target[col + target_first, 8 * g : 8 * g + 8, :] = total[g]
            return carry

        lax.fori_loop(0, COLS, column, 0)

    def to_blocks(source, first, target):
        for x in range(2):
            for g in range(ROWS // 8):
                columns = [source[first + 4 * x + i, 8 * g : 8 * g + 8, :] for i in range(4)]
                for y, value in enumerate(regroup(columns, lane)):
                    target[0, x, y, 8 * g : 8 * g + 8, :] = value

    shift_columns(wide, end_in)
    apply(wide, prev_t, 0, wide2.at[0], RIM)
    pack_ends(wide2, end_out2, False)
    copies = exchange(1, wide2, end_out2, end_in2)
    to_blocks(wide2.at[0], RIM, first_ref)
    for copy in copies:
        copy.wait()
    shift_columns(wide2, end_in2)
    apply(wide2, wide.at[0], RIM, prev_t, 0)
    to_blocks(prev_t, 0, second_ref)


def body(prev_vec, cur_vec, displace, potential):
    f32 = jnp.float32
    vmem = pl.BlockSpec(memory_space=pltpu.VMEM)
    return pl.pallas_call(
        kernel,
        out_shape=(jax.ShapeDtypeStruct(cur_vec.shape, f32),) * 2,
        in_specs=[pl.BlockSpec(memory_space=pl.ANY)] * 4,
        out_specs=(vmem, vmem),
        scratch_shapes=[
            pltpu.VMEM(prev_vec.shape, f32),
            pltpu.VMEM(cur_vec.shape, f32),
            pltpu.VMEM(displace.shape, f32),
            pltpu.VMEM(potential.shape, f32),
            pltpu.VMEM((2, 4, 8, 128), f32),
            pltpu.VMEM((COLS, ROWS, 128), f32),
            pltpu.VMEM((2, WIDE, FULL, 128), f32),
            pltpu.VMEM((2, WIDE, ROWS, 128), f32),
            pltpu.VMEM((2, 16, 128), f32),
            pltpu.VMEM((2, 2, 3, 16, 128), f32),
            pltpu.VMEM((2, 8, 128), f32),
            pltpu.VMEM((2, 2, 3, 8, 128), f32),
            pltpu.VMEM((2, 2 * STEPS + 1, WIDE, ROWS, 128), f32),
            pltpu.VMEM((2, 2, 16, 128), f32),
            pltpu.VMEM((2, 2, 16, 128), f32),
            pltpu.VMEM((2, 2 * STEPS + 1, 16, 128), f32),
            pltpu.VMEM((2, 2 * STEPS + 1, 16, 128), f32),
            pltpu.VMEM((len(PLANE), COLS, 128), f32),
            pltpu.VMEM((len(INTER), COLS, 128), f32),
            pltpu.SemaphoreType.DMA((4,)),
            pltpu.SemaphoreType.DMA((2, len(PEERS))),
            pltpu.SemaphoreType.DMA((2, len(PEERS))),
        ],
        compiler_params=pltpu.CompilerParams(
            collective_id=0, has_side_effects=True, vmem_limit_bytes=24 * 1024 * 1024
        ),
        name="two_terms",
    )(prev_vec, cur_vec, displace, potential)


def solution(mesh):
    in_specs = (
        P("layer", "gx", "gy", None, None),
        P("layer", "gx", "gy", None, None),
        P("layer", "gx", "gy", None, None),
        P("layer", "gx", "gy", None),
    )
    out_specs = (P("layer", "gx", "gy", None, None), P("layer", "gx", "gy", None, None))
    return jax.shard_map(body, mesh=mesh, in_specs=in_specs, out_specs=out_specs, check_vma=False)
```

profile of v0, /device:TPU:16, one launch (start us, length us, event | category | flops | bytes accessed | tf_op | source)
XLA Modules:
  0.0 46.0 jit_solution(14972093943325869354)
XLA Ops:
  0.6 0.0 copy-start
  0.6 0.9 %copy-done = f32[1,2,4,32,128]{4,3,2,1,0:T(8,128)S(1)} copy-done((f32[1,2,4,32,128]{4,3,2,1,0:T(8,128)S(1)}, f32[1,2,4,32,128]{4,3,2,1,0:T(8,128)}, u32[]{:S(2)}) %copy-start) | copy-done | bytes 131096
  1.5 0.0 copy-start.1
  1.5 0.9 %copy-done.1 = f32[1,2,4,32,128]{4,3,2,1,0:T(8,128)S(1)} copy-done((f32[1,2,4,32,128]{4,3,2,1,0:T(8,128)S(1)}, f32[1,2,4,32,128]{4,3,2,1,0:T(8,128)}, u32[]{:S(2)}) %copy-start.1) | copy-done | bytes 131096
  2.4 0.0 copy-start.2
  2.4 0.7 %copy-done.2 = f32[1,2,4,2,128]{4,3,2,1,0:T(2,128)S(1)} copy-done((f32[1,2,4,2,128]{4,3,2,1,0:T(2,128)S(1)}, f32[1,2,4,2,128]{4,3,2,1,0:T(2,128)}, u32[]{:S(2)}) %copy-start.2) | copy-done | bytes 8216
  3.1 0.0 copy-start.3
  3.1 0.7 %copy-done.3 = f32[1,2,4,128]{3,2,1,0:T(4,128)S(1)} copy-done((f32[1,2,4,128]{3,2,1,0:T(4,128)S(1)}, f32[1,2,4,128]{3,2,1,0:T(4,128)}, u32[]{:S(2)}) %copy-start.3) | copy-done | bytes 4120
  3.8 40.9 %two_terms.1 = (f32[1,2,4,32,128]{4,3,2,1,0:T(8,128)S(1)}, f32[1,2,4,32,128]{4,3,2,1,0:T(8,128)S(1)}) custom-call(f32[1,2,4,32,128]{4,3,2,1,0:T(8,128)S(1)} %copy-done, f32[1,2,4,32,128]{4,3,2,1,0:T(8,128)S(1)} %copy-done.1, f32[1,2,4,2,128]{4,3,2,1,0:T(2,128)S(1)} %copy-done.2, f32[1,2,4,128]{3,2,1,0:T(4,128)S(1)} %copy-done.3), custom_call_target="tpu_custom_call" | custom-call | tf_op jit(solution)/shard_map/two_terms/pallas_call | solution.py:370
  44.7 0.7 %copy.8 = f32[1,2,4,32,128]{4,3,2,1,0:T(8,128)} copy(f32[1,2,4,32,128]{4,3,2,1,0:T(8,128)S(1)} %get-tuple-element.4) | data formatting | bytes 262144
  45.4 0.7 %copy.9 = f32[1,2,4,32,128]{4,3,2,1,0:T(8,128)} copy(f32[1,2,4,32,128]{4,3,2,1,0:T(8,128)S(1)} %get-tuple-element.5) | data formatting | bytes 262144
Async XLA Ops:
  0.6 0.9 %copy-start = (f32[1,2,4,32,128]{4,3,2,1,0:T(8,128)S(1)}, f32[1,2,4,32,128]{4,3,2,1,0:T(8,128)}, u32[]{:S(2)}) copy-start(f32[1,2,4,32,128]{4,3,2,1,0:T(8,128)} %prev_hbm.1) | copy-start | bytes 393220
  1.5 0.9 %copy-start.1 = (f32[1,2,4,32,128]{4,3,2,1,0:T(8,128)S(1)}, f32[1,2,4,32,128]{4,3,2,1,0:T(8,128)}, u32[]{:S(2)}) copy-start(f32[1,2,4,32,128]{4,3,2,1,0:T(8,128)} %cur_hbm.1) | copy-start | bytes 393220
  2.4 0.7 %copy-start.2 = (f32[1,2,4,2,128]{4,3,2,1,0:T(2,128)S(1)}, f32[1,2,4,2,128]{4,3,2,1,0:T(2,128)}, u32[]{:S(2)}) copy-start(f32[1,2,4,2,128]{4,3,2,1,0:T(2,128)} %disp_hbm.1) | copy-start | bytes 24580
  3.1 0.7 %copy-start.3 = (f32[1,2,4,128]{3,2,1,0:T(4,128)S(1)}, f32[1,2,4,128]{3,2,1,0:T(4,128)}, u32[]{:S(2)}) copy-start(f32[1,2,4,128]{3,2,1,0:T(4,128)} %pot_hbm.1) | copy-start | bytes 12292
where the time goes:
time: 46.3 us; the launch traced here: 46 us
  Pallas kernels  40.9 us (88%)
  local copies, waits for them, and re-layouts  4.5 us (10%)
  between operations  0.65 us (1%)
    pallas_call x1, Pallas kernels, body(): pl.pallas_call(kernel, out_shape=(jax.ShapeDtypeStruct(cur_vec.shape, f32...  40.9 us
    unnamed x10, local copies, waits for them, and re-layouts  4.5 us

commit v1 on v0

v1 whole, which is shorter than its diff:
```python
import math

import jax
import jax.numpy as jnp
import numpy as np
from jax import lax
from jax.experimental import pallas as pl
from jax.experimental.pallas import tpu as pltpu
from jax.sharding import PartitionSpec as P

MESH = pl.DeviceIdType.MESH
PATCH_X = 14
PATCH_Y = 4

v_pi = -2.7
v_sigma = 0.48
decay_len = 0.319
layer_gap = 3.35 / 1.42
cut_radius = 3.5
hop_scale = 12.0
twist_angle = 1.05 * math.pi / 180.0
root_three = math.sqrt(3.0)
cell_w = 4.0 * root_three
cell_h = 24.0
reach = 0.15

COLS = 8
RIM = 2
WIDE = COLS + 2 * RIM
STEPS = 5
ROWS = 32
GROUP = 4
atom_x = (0.0, root_three / 2.0, root_three / 2.0, 0.0)
atom_y = (0.0, 0.5, 1.5, 2.0)


def near_offsets():
    cos_t, sin_t = math.cos(twist_angle), math.sin(twist_angle)
    cells = []
    for s in range(4):
        col, row = np.meshgrid(np.arange(4 * PATCH_X), np.arange(8 * PATCH_Y), indexing="ij")
        x = (col - 2 * PATCH_X) * root_three + atom_x[s]
        y = (row - 4 * PATCH_Y) * 3.0 + atom_y[s]
        cells.append(np.stack([x.ravel(), y.ravel()], -1))
    places = np.concatenate(cells)
    turn = np.array([[cos_t - 1.0, -sin_t], [sin_t, cos_t - 1.0]])
    drift = places @ turn.T
    drift = np.concatenate([drift, -drift])
    slack = 2.0 * reach + 1e-3
    flat = math.sqrt(cut_radius**2 - layer_gap**2)
    plane, inter = [], []
    for step in range(-STEPS - 2, STEPS + 3):
        for col in range(-RIM - 2, RIM + 3):
            hit_plane = hit_inter = False
            for s in range(4):
                t = (s + step) % 4
                x = atom_x[s] - atom_x[t] - col * root_three
                y = atom_y[s] - atom_y[t] - 3.0 * ((s + step) // 4)
                hit_plane |= math.hypot(x, y) - slack * math.sqrt(2.0) < cut_radius
                gap = np.maximum(np.abs(np.array([x, y]) + drift) - slack, 0.0)
                hit_inter |= bool((np.hypot(gap[:, 0], gap[:, 1]) < flat).any())
            if hit_plane and (col, step) != (0, 0):
                plane.append((col, step))
            if hit_inter:
                inter.append((col, step))
    assert max(abs(c) for c, _ in plane + inter) <= RIM
    assert max(abs(s) for _, s in plane + inter) <= STEPS
    return plane, inter


PLANE, INTER = near_offsets()
TILE = (1, 0, 0)
SIDES = [(a, b, 0) for a in (0, 1) for b in (-1, 1)]
ENDS = [(a, 0, c) for a in (0, 1) for c in (-1, 1)]
CORNERS = [(a, b, c) for a in (0, 1) for b in (-1, 1) for c in (-1, 1)]
PEERS = SIDES + [TILE] + ENDS
MESSAGES = 40
VMEM_LIMIT = 62 * 1024 * 1024


def peer(step):
    sizes = [lax.axis_size(a) for a in ("layer", "gx", "gy")]
    return tuple(
        lax.rem(lax.axis_index(a) + s + n, n) for a, s, n in zip(("layer", "gx", "gy"), step, sizes)
    )


def pick(index, table):
    value = jnp.full(index.shape, table[3], jnp.float32)
    for s in range(3):
        value = jnp.where(index == s, jnp.float32(table[s]), value)
    return value


def regroup(parts, lane):
    group = lane // 32
    results = []
    for a in range(4):
        value = parts[a]
        for b in range(4):
            if b != a:
                value = jnp.where(group == b, pltpu.roll(parts[b], (32 * (b - a)) % 128, 1), value)
        results.append(value)
    return results


def kernel(
    prev_hbm, cur_hbm, disp_hbm, pot_hbm, result,
    prev_in, cur_in, disp_in, pot_in, pot_t, prev_t, second_t, wide, wide2,
    end_out, end_in, end_out2, end_in2, spot_in,
    rims, spot, spot_rim, near_plane, near_inter, own_spot, hop_plane, hop_inter,
    load_sem, send_sem, recv_sem,
):
    barrier = pltpu.get_barrier_semaphore()
    for step in PEERS:
        pl.semaphore_signal(barrier, inc=1, device_id=peer(step), device_id_type=MESH)
    loads = [
        pltpu.make_async_copy(src, dst, load_sem.at[i])
        for i, (src, dst) in enumerate(
            ((disp_hbm, disp_in), (cur_hbm, cur_in), (prev_hbm, prev_in), (pot_hbm, pot_in))
        )
    ]
    for load in loads:
        load.start()
    lane = lax.broadcasted_iota(jnp.int32, (8, 128), 1)
    zero = jnp.zeros((8, 128), jnp.float32)
    sent = []

    def send(source, target, step):
        n = len(sent)
        copy = pltpu.make_async_remote_copy(
            src_ref=source,
            dst_ref=target,
            send_sem=send_sem.at[n],
            recv_sem=recv_sem.at[n],
            device_id=peer(step),
            device_id_type=MESH,
        )
        copy.start()
        sent.append(copy)
        return copy

    def send_side(buffer, layer, gx):
        source, target = (COLS, 0) if gx > 0 else (RIM, RIM + COLS)
        return send(
            buffer.at[0, pl.ds(source, RIM)], buffer.at[layer, pl.ds(target, RIM)], (layer, gx, 0)
        )

    def send_tile(buffer, first, count):
        where = pl.ds(RIM + first, count)
        return send(buffer.at[0, where], buffer.at[1, where], TILE)

    def send_end(source, target, step):
        layer, gx, gy = step
        end = 0 if gy > 0 else 1
        return send(source.at[end], target.at[1 - gx, layer, end], step)

    def to_columns(source, target, first):
        for x in range(2):
            for g in range(ROWS // 8):
                parts = [source[0, x, y, 8 * g : 8 * g + 8, :] for y in range(4)]
                for i, value in enumerate(regroup(parts, lane)):
                    target[first + 4 * x + i, 8 * g : 8 * g + 8, :] = value

    def pack_ends(source, target):
        low, high = zero, zero
        for k in range(32):
            value = source[0, RIM + k // 4, 8 * (k % 4) : 8 * (k % 4) + 8, :]
            value = pltpu.roll(value, (4 * k + 4) % 128, 1)
            low = jnp.where(lane // 4 == k, value, low)
            high = jnp.where(lane // 4 == (k + 1) % 32, value, high)
        target[0, 0:8, :] = low
        target[1, 0:8, :] = high

    loads[0].wait()
    for x in range(2):
        for i, value in enumerate(regroup([disp_in[0, x, y] for y in range(4)], lane[:2])):
            for axis in range(2):
                spot_in[1, 0, axis, 4 * x + i : 4 * x + i + 1, :] = value[axis : axis + 1]
    for end in range(2):
        end_out[end, 8:16, :] = spot_in[1, 0, 0]
        end_out[end, 16:24, :] = spot_in[1, 0, 1]
    loads[1].wait()
    to_columns(cur_in, wide.at[0], RIM)
    pack_ends(wide, end_out)

    pl.semaphore_wait(barrier, len(PEERS))
    ends = [send_end(end_out, end_in, step) for step in ENDS]
    spots = [send(spot_in.at[1, 0], spot_in.at[1 - gx, layer], (layer, gx, gy)) for layer, gx, gy in SIDES + [TILE]]
    right_rim = [send_side(wide, layer, -1) for layer in (1, 0)]
    right_tile = send_tile(wide, 2, COLS - 2)
    left_rim = [send_side(wide, layer, 1) for layer in (1, 0)]
    left_tile = send_tile(wide, 0, 2)

    loads[2].wait()
    to_columns(prev_in, prev_t, 0)
    loads[3].wait()
    for x in range(2):
        for i, value in enumerate(regroup([pot_in[0, x, y : y + 1] for y in range(4)], lane[:1])):
            pot_t[4 * x + i : 4 * x + i + 1, :] = value

    for copy in ends:
        copy.wait_recv()
    corners = [send(end_in.at[1], end_in.at[1 - gx], (0, gx, 0)) for gx in (-1, 1)]
    for copy in spots + corners:
        copy.wait_recv()

    def rim_of(col):
        side = 0 if col < RIM else (1 if col < RIM + COLS else 2)
        return side, (col + COLS - RIM) % COLS

    def end_levels(low, high, k):
        picked = jnp.where(((lane + (124 - 4 * k)) & 127) < 64, high, low)
        return pltpu.roll(picked, 124 - 4 * k, 1)

    def with_rim(sides):
        return jnp.concatenate([sides[0][COLS - RIM :], sides[1], sides[2][:RIM], zero[:4]], axis=0)

    for layer in range(2):
        for axis in range(2):
            spot[layer, axis] = with_rim([spot_in[side, layer, axis] for side in range(3)])
            rows = slice(8 + 8 * axis, 16 + 8 * axis)
            spot_rim[layer, axis] = with_rim([
                jnp.where(lane < 64, end_in[side, layer, 1, rows, :], end_in[side, layer, 0, rows, :])
                for side in range(3)
            ])

    layer_id = lax.axis_index("layer")
    cos_t, sin_t = math.cos(twist_angle), math.sin(twist_angle)
    upper = layer_id == 1
    cos_own = jnp.where(upper, jnp.float32(cos_t), jnp.float32(1.0))
    sin_own = jnp.where(upper, jnp.float32(sin_t), jnp.float32(0.0))

    row16 = lax.broadcasted_iota(jnp.int32, (16, 128), 0)
    lane16 = lax.broadcasted_iota(jnp.int32, (16, 128), 1)
    atom = lane16 & 3
    block = (lax.axis_index("gx") * 2 + (row16 + RIM) // 4 - 1 + 2 * lax.axis_size("gx")) % (
        2 * lax.axis_size("gx")
    )
    at_x = (
        ((row16 + RIM) & 3).astype(jnp.float32) * root_three
        + pick(atom, atom_x)
        - cell_w / 2.0
        + cell_w * ((block % PATCH_X).astype(jnp.float32) - (PATCH_X - 1) / 2.0)
    )
    at_y = (
        ((lane16 // 4) & 7).astype(jnp.float32) * 3.0
        + pick(atom, atom_y)
        - cell_h / 2.0
        + cell_h * ((lane16 // 32).astype(jnp.float32) - (PATCH_Y - 1) / 2.0)
    )
    turn_x = (cos_t - 1.0) * at_x - sin_t * at_y
    turn_y = sin_t * at_x + (cos_t - 1.0) * at_y
    own_on = jnp.where(upper, jnp.float32(1.0), jnp.float32(0.0))
    other_on = 1.0 - own_on

    def unturned(ref):
        return (
            cos_own * ref[0, 0] + sin_own * ref[0, 1],
            cos_own * ref[0, 1] - sin_own * ref[0, 0],
        )

    plane_here, plane_rim = unturned(spot), unturned(spot_rim)
    turns = (turn_x, turn_y)

    def joined(here, rim, step, lanes):
        if step > 0:
            return jnp.where(lanes < step, rim, here)
        if step < 0:
            return jnp.where(lanes >= 128 + step, rim, here)
        return here

    def rolled_by(value, step):
        return pltpu.roll(value, step % 128, 1) if step else value

    inner = slice(RIM, RIM + COLS)
    for axis in range(2):
        near_plane[axis, 0] = plane_here[axis]
        near_plane[axis, 1] = plane_rim[axis]
        near_inter[axis, 0] = spot[1, axis] + other_on * turns[axis]
        near_inter[axis, 1] = spot_rim[1, axis] + other_on * turns[axis]
        own_spot[axis] = near_plane[axis, 0, inner, :]
        own_spot[2 + axis] = spot[0, axis, inner, :] + own_on * turns[axis][inner]

    def atom_heights(index):
        return (index >> 2).astype(jnp.float32) * 3.0 + pick(index & 3, atom_y)

    log2e = 1.0 / math.log(2.0)
    inverse_cut = 1.0 / (cut_radius * cut_radius)
    scale = 2.0 / hop_scale
    sigma_part = v_sigma * math.exp((layer_gap - 1.0) / decay_len)

    def parts(first, near, col, step):
        base_x = pick((lane - step + 8) & 3, atom_x) - pick(lane & 3, atom_x)
        base_y = atom_heights(lane - step + 8) - atom_heights(lane + 8)
        rows = slice(RIM + col, RIM + col + COLS)
        own = [rolled_by(own_spot[first + axis], step) for axis in range(2)]
        other = [joined(near[axis, 0, rows, :], near[axis, 1, rows, :], step, lane) for axis in range(2)]
        delta_x = (own[0] - other[0]) + (base_x - col * root_three)
        delta_y = (own[1] - other[1]) + base_y
        return delta_x * delta_x + delta_y * delta_y

    def envelope(dist_sq, inverse):
        spread = dist_sq * inverse
        fall = jnp.exp2(spread * (-log2e / decay_len) + log2e / decay_len)
        scaled = dist_sq * inverse_cut
        return fall * jnp.maximum(1.0 - scaled * scaled, 0.0)

    for n, (col, step) in enumerate(PLANE):
        dist_sq = parts(0, near_plane, col, step)
        hop_plane[n] = envelope(dist_sq, lax.rsqrt(dist_sq)) * (v_pi * scale)
    for n, (col, step) in enumerate(INTER):
        dist_sq = parts(2, near_inter, col, step) + layer_gap * layer_gap
        inverse = lax.rsqrt(dist_sq)
        cosine_sq = (inverse * inverse) * (layer_gap * layer_gap)
        mix = cosine_sq * ((sigma_part - v_pi) * scale) + v_pi * scale
        hop_inter[n] = envelope(dist_sq, inverse) * mix

    def unpack_ends(ends):
        for layer in range(2):
            for col in range(WIDE):
                side, own = rim_of(col)
                for g in range(4):
                    low, high = ends[side, layer, 0, 0:8, :], ends[side, layer, 1, 0:8, :]
                    rims[layer, col, 8 * g : 8 * g + 8, :] = end_levels(low, high, own * 4 + g)

    def apply(buffer, minus, minus_first, target, target_first, first, count):
        def columns(group, carry):
            base = group * GROUP
            total = {}
            for d in range(GROUP):
                onsite = jnp.broadcast_to(pot_t[pl.ds(base + d, 1), :] * scale, (8, 128))
                for g in range(4):
                    rows = slice(8 * g, 8 * g + 8)
                    total[d, g] = (
                        onsite * buffer[0, base + d + RIM, rows, :] - minus[base + d + minus_first, rows, :]
                    )
            for step in range(-STEPS, STEPS + 1):
                part = {}
                for layer, (offsets, hops) in enumerate(((PLANE, hop_plane), (INTER, hop_inter))):
                    here = [(n, dcol) for n, (dcol, s) in enumerate(offsets) if s == step]
                    weight = {
                        (n, d): jnp.broadcast_to(hops[n, pl.ds(base + d, 1), :], (8, 128))
                        for n, _ in here
                        for d in range(GROUP)
                    }
                    for c in range(GROUP + 2 * RIM):
                        users = [(n, c - RIM - dcol) for n, dcol in here if 0 <= c - RIM - dcol < GROUP]
                        for g in range(4):
                            rows = slice(8 * g, 8 * g + 8)
                            near = buffer[layer, base + c, rows, :]
                            if step:
                                near = joined(near, rims[layer, base + c, rows, :], step, lane)
                            for n, d in users:
                                term = weight[n, d] * near
                                part[d, g] = part[d, g] + term if (d, g) in part else term
                for key, value in part.items():
                    total[key] = total[key] + rolled_by(value, -step)
            for (d, g), value in total.items():
                target[base + d + target_first, 8 * g : 8 * g + 8, :] = value
            return carry

        lax.fori_loop(first // GROUP, (first + count) // GROUP, columns, 0)

    def to_blocks(source, first, n):
        for x in range(2):
            for g in range(ROWS // 8):
                columns = [source[first + 4 * x + i, 8 * g : 8 * g + 8, :] for i in range(4)]
                for y, value in enumerate(regroup(columns, lane)):
                    result[n, 0, x, y, 8 * g : 8 * g + 8, :] = value

    half = COLS // 2
    unpack_ends(end_in)
    for copy in right_rim + [right_tile]:
        copy.wait_recv()
    apply(wide, prev_t, 0, wide2.at[0], RIM, half, half)
    last = [send_side(wide2, layer, 1) for layer in (1, 0)]
    last.append(send_tile(wide2, half, half))
    for copy in left_rim + [left_tile]:
        copy.wait_recv()
    apply(wide, prev_t, 0, wide2.at[0], RIM, 0, half)
    pack_ends(wide2, end_out2)
    last += [send_end(end_out2, end_in2, step) for step in ENDS + CORNERS]
    last += [send_side(wide2, layer, -1) for layer in (1, 0)]
    last.append(send_tile(wide2, 0, half))
    to_blocks(wide2.at[0], RIM, 0)
    for copy in last:
        copy.wait_recv()
    unpack_ends(end_in2)
    apply(wide2, wide.at[0], RIM, second_t, 0, 0, COLS)
    to_blocks(second_t, 0, 1)
    for copy in sent:
        copy.wait_send()


def finish(result, first_ref, second_ref):
    first_ref[...] = result[0]
    second_ref[...] = result[1]


def body(prev_vec, cur_vec, displace, potential):
    f32 = jnp.float32
    near = pltpu.VMEM((2, 2, 16, 128), f32)
    hbm, vmem = pl.BlockSpec(memory_space=pltpu.HBM), pl.BlockSpec(memory_space=pltpu.VMEM)
    result = pl.pallas_call(
        kernel,
        out_shape=jax.ShapeDtypeStruct((2,) + cur_vec.shape, f32),
        in_specs=[hbm] * 4,
        out_specs=pl.BlockSpec(memory_space=pltpu.VMEM),
        scratch_shapes=[
            pltpu.VMEM(prev_vec.shape, f32),
            pltpu.VMEM(cur_vec.shape, f32),
            pltpu.VMEM(displace.shape, f32),
            pltpu.VMEM(potential.shape, f32),
            pltpu.VMEM((COLS, 128), f32),
            pltpu.VMEM((COLS, ROWS, 128), f32),
            pltpu.VMEM((COLS, ROWS, 128), f32),
            pltpu.VMEM((2, WIDE, ROWS, 128), f32),
            pltpu.VMEM((2, WIDE, ROWS, 128), f32),
            pltpu.VMEM((2, 24, 128), f32),
            pltpu.VMEM((3, 2, 2, 24, 128), f32),
            pltpu.VMEM((2, 8, 128), f32),
            pltpu.VMEM((3, 2, 2, 8, 128), f32),
            pltpu.VMEM((3, 2, 2, COLS, 128), f32),
            pltpu.VMEM((2, WIDE, ROWS, 128), f32),
            near,
            near,
            near,
            near,
            pltpu.VMEM((4, COLS, 128), f32),
            pltpu.VMEM((len(PLANE), COLS, 128), f32),
            pltpu.VMEM((len(INTER), COLS, 128), f32),
            pltpu.SemaphoreType.DMA((4,)),
            pltpu.SemaphoreType.DMA((MESSAGES,)),
            pltpu.SemaphoreType.DMA((MESSAGES,)),
        ],
        compiler_params=pltpu.CompilerParams(
            collective_id=0, has_side_effects=True, vmem_limit_bytes=VMEM_LIMIT
        ),
        name="two_terms",
    )(prev_vec, cur_vec, displace, potential)
    return pl.pallas_call(
        finish,
        out_shape=(jax.ShapeDtypeStruct(cur_vec.shape, f32),) * 2,
        in_specs=[vmem],
        out_specs=(vmem, vmem),
        name="finish",
    )(result)


def solution(mesh):
    in_specs = (
        P("layer", "gx", "gy", None, None),
        P("layer", "gx", "gy", None, None),
        P("layer", "gx", "gy", None, None),
        P("layer", "gx", "gy", None),
    )
    out_specs = (P("layer", "gx", "gy", None, None), P("layer", "gx", "gy", None, None))
    return jax.shard_map(body, mesh=mesh, in_specs=in_specs, out_specs=out_specs, check_vma=False)
```

time: 46.3 us -> 34.1 us (0.74)
  the two profiles are of different devices: /device:TPU:16 before, /device:TPU:1 now
where the time goes in v1:
time: 34.1 us; the launch traced here: 33.9 us
  Pallas kernels  33.3 us (98%)
  between operations  0.64 us (2%)
    pallas_call x1, Pallas kernels, body(): pl.pallas_call(kernel, out_shape=jax.ShapeDtypeStruct((2,) + cur_vec.shap...  31.6 us
    pallas_call x1, Pallas kernels, body(): pl.pallas_call(finish, out_shape=(jax.ShapeDtypeStruct(cur_vec.shape, f32...  1.66 us

profile of v1, /device:TPU:1, one launch (start us, length us, event | category | flops | bytes accessed | tf_op | source)
XLA Modules:
  0.0 33.9 jit_solution(16085942767405072019)
XLA Ops:
  0.6 31.6 %two_terms.1.result = f32[2,1,2,4,32,128]{5,4,3,2,1,0:T(8,128)} custom-call(f32[1,2,4,32,128]{4,3,2,1,0:T(8,128)} %prev_hbm.1, f32[1,2,4,32,128]{4,3,2,1,0:T(8,128)} %cur_hbm.1, f32[1,2,4,2,128]{4,3,2,1,0:T(2,128)} %disp_hbm.1, f32[1,2,4,128]{3,2,1,0:T(4,128)} %pot_hbm.1), custom_call_target="tpu_custom_call" | custom-call | tf_op jit(solution)/shard_map/two_terms/pallas_call | solution.py:405
  32.2 1.7 %finish.1 = (f32[1,2,4,32,128]{4,3,2,1,0:T(8,128)}, f32[1,2,4,32,128]{4,3,2,1,0:T(8,128)}) custom-call(f32[2,1,2,4,32,128]{5,4,3,2,1,0:T(8,128)} %two_terms.1.result), custom_call_target="tpu_custom_call" | custom-call | tf_op jit(solution)/shard_map/finish/pallas_call | solution.py:442

commit v2 on v1

--- a/solution.py
+++ b/solution.py
@@ -73,9 +73,11 @@
 SIDES = [(a, b, 0) for a in (0, 1) for b in (-1, 1)]
 ENDS = [(a, 0, c) for a in (0, 1) for c in (-1, 1)]
 CORNERS = [(a, b, c) for a in (0, 1) for b in (-1, 1) for c in (-1, 1)]
-PEERS = SIDES + [TILE] + ENDS
-MESSAGES = 40
-VMEM_LIMIT = 62 * 1024 * 1024
+LEFT = [(a, -1, 0) for a in (0, 1)]
+RIGHT = [(a, 1, 0) for a in (0, 1)]
+PEERS = [TILE] + ENDS
+MESSAGES = 41
+VMEM_LIMIT = 40 * 1024 * 1024
 
 
 def peer(step):
@@ -109,10 +111,10 @@
     prev_in, cur_in, disp_in, pot_in, pot_t, prev_t, second_t, wide, wide2,
     end_out, end_in, end_out2, end_in2, spot_in,
     rims, spot, spot_rim, near_plane, near_inter, own_spot, hop_plane, hop_inter,
-    load_sem, send_sem, recv_sem,
+    load_sem, send_sem, recv_sem, corner_sem, left_sem,
 ):
     barrier = pltpu.get_barrier_semaphore()
-    for step in PEERS:
+    for step in PEERS + LEFT:
         pl.semaphore_signal(barrier, inc=1, device_id=peer(step), device_id_type=MESH)
     loads = [
         pltpu.make_async_copy(src, dst, load_sem.at[i])
@@ -128,6 +130,7 @@
 
     def send(source, target, step):
         n = len(sent)
+        assert n < MESSAGES
         copy = pltpu.make_async_remote_copy(
             src_ref=source,
             dst_ref=target,
@@ -162,15 +165,16 @@
                 for i, value in enumerate(regroup(parts, lane)):
                     target[first + 4 * x + i, 8 * g : 8 * g + 8, :] = value
 
-    def pack_ends(source, target):
-        low, high = zero, zero
-        for k in range(32):
+    def pack_ends(source, targets, columns, ends=None):
+        low, high = ends or (zero, zero)
+        for k in range(4 * columns.start, 4 * columns.stop):
             value = source[0, RIM + k // 4, 8 * (k % 4) : 8 * (k % 4) + 8, :]
             value = pltpu.roll(value, (4 * k + 4) % 128, 1)
             low = jnp.where(lane // 4 == k, value, low)
             high = jnp.where(lane // 4 == (k + 1) % 32, value, high)
-        target[0, 0:8, :] = low
-        target[1, 0:8, :] = high
+        targets[0, 0:8, :] = low
+        targets[1, 0:8, :] = high
+        return low, high
 
     loads[0].wait()
     for x in range(2):
@@ -178,19 +182,37 @@
             for axis in range(2):
                 spot_in[1, 0, axis, 4 * x + i : 4 * x + i + 1, :] = value[axis : axis + 1]
     for end in range(2):
-        end_out[end, 8:16, :] = spot_in[1, 0, 0]
-        end_out[end, 16:24, :] = spot_in[1, 0, 1]
+        moved = pltpu.roll(spot_in[1, 0, 1], 4 if end else 124, 1)
+        keep = lane < 4 if end else lane >= 124
+        end_out[end, 8:16, :] = jnp.where(keep, spot_in[1, 0, 0], moved)
     loads[1].wait()
     to_columns(cur_in, wide.at[0], RIM)
-    pack_ends(wide, end_out)
-
-    pl.semaphore_wait(barrier, len(PEERS))
-    ends = [send_end(end_out, end_in, step) for step in ENDS]
-    spots = [send(spot_in.at[1, 0], spot_in.at[1 - gx, layer], (layer, gx, gy)) for layer, gx, gy in SIDES + [TILE]]
-    right_rim = [send_side(wide, layer, -1) for layer in (1, 0)]
+    pack_ends(wide, end_out, range(COLS))
+
+    def tell(sem, steps):
+        for step in steps:
+            pl.semaphore_signal(sem, inc=1, device_id=peer(step), device_id_type=MESH)
+
+    def send_spots(steps):
+        return [send(spot_in.at[1, 0], spot_in.at[1 - gx, layer], (layer, gx, gy)) for layer, gx, gy in steps]
+
+    pl.semaphore_wait(barrier, len(PEERS + RIGHT))
+    tell(left_sem, RIGHT)
+    tell(corner_sem.at[0], [(0, 0, -1), (0, 0, 1)])
+    near_right = [send_end(end_out, end_in, step) for step in ENDS]
+    near_right += send_spots([TILE])
+    near_left = send_spots(RIGHT)
     right_tile = send_tile(wide, 2, COLS - 2)
     left_rim = [send_side(wide, layer, 1) for layer in (1, 0)]
     left_tile = send_tile(wide, 0, 2)
+    pl.semaphore_wait(corner_sem.at[0], 2)
+    near_left += [send_end(end_out, end_in, step) for step in CORNERS if step[1] > 0]
+    pl.semaphore_wait(left_sem, 2)
+    tell(corner_sem.at[1], [(0, 0, -1), (0, 0, 1)])
+    near_right += send_spots(LEFT)
+    right_rim = [send_side(wide, layer, -1) for layer in (1, 0)]
+    pl.semaphore_wait(corner_sem.at[1], 2)
+    near_right += [send_end(end_out, end_in, step) for step in CORNERS if step[1] < 0]
 
     loads[2].wait()
     to_columns(prev_in, prev_t, 0)
@@ -199,12 +221,6 @@
         for i, value in enumerate(regroup([pot_in[0, x, y : y + 1] for y in range(4)], lane[:1])):
             pot_t[4 * x + i : 4 * x + i + 1, :] = value
 
-    for copy in ends:
-        copy.wait_recv()
-    corners = [send(end_in.at[1], end_in.at[1 - gx], (0, gx, 0)) for gx in (-1, 1)]
-    for copy in spots + corners:
-        copy.wait_recv()
-
     def rim_of(col):
         side = 0 if col < RIM else (1 if col < RIM + COLS else 2)
         return side, (col + COLS - RIM) % COLS
@@ -216,14 +232,11 @@
     def with_rim(sides):
         return jnp.concatenate([sides[0][COLS - RIM :], sides[1], sides[2][:RIM], zero[:4]], axis=0)
 
-    for layer in range(2):
-        for axis in range(2):
-            spot[layer, axis] = with_rim([spot_in[side, layer, axis] for side in range(3)])
-            rows = slice(8 + 8 * axis, 16 + 8 * axis)
-            spot_rim[layer, axis] = with_rim([
-                jnp.where(lane < 64, end_in[side, layer, 1, rows, :], end_in[side, layer, 0, rows, :])
-                for side in range(3)
-            ])
+    def end_spot(side, layer, axis):
+        low, high = end_in[side, layer, 0, 8:16, :], end_in[side, layer, 1, 8:16, :]
+        if axis:
+            low, high = pltpu.roll(low, 4, 1), pltpu.roll(high, 124, 1)
+        return jnp.where(lane < 64, high, low)
 
     layer_id = lax.axis_index("layer")
     cos_t, sin_t = math.cos(twist_angle), math.sin(twist_angle)
@@ -260,7 +273,6 @@
             cos_own * ref[0, 1] - sin_own * ref[0, 0],
         )
 
-    plane_here, plane_rim = unturned(spot), unturned(spot_rim)
     turns = (turn_x, turn_y)
 
     def joined(here, rim, step, lanes):
@@ -274,13 +286,24 @@
         return pltpu.roll(value, step % 128, 1) if step else value
 
     inner = slice(RIM, RIM + COLS)
-    for axis in range(2):
-        near_plane[axis, 0] = plane_here[axis]
-        near_plane[axis, 1] = plane_rim[axis]
-        near_inter[axis, 0] = spot[1, axis] + other_on * turns[axis]
-        near_inter[axis, 1] = spot_rim[1, axis] + other_on * turns[axis]
-        own_spot[axis] = near_plane[axis, 0, inner, :]
-        own_spot[2 + axis] = spot[0, axis, inner, :] + own_on * turns[axis][inner]
+    def find_spots(sides):
+        blank = [zero] * 3
+        for layer in range(2):
+            for axis in range(2):
+                here, rim = list(blank), list(blank)
+                for side in sides:
+                    here[side] = spot_in[side, layer, axis]
+                    rim[side] = end_spot(side, layer, axis)
+                spot[layer, axis] = with_rim(here)
+                spot_rim[layer, axis] = with_rim(rim)
+        plane_here, plane_rim = unturned(spot), unturned(spot_rim)
+        for axis in range(2):
+            near_plane[axis, 0] = plane_here[axis]
+            near_plane[axis, 1] = plane_rim[axis]
+            near_inter[axis, 0] = spot[1, axis] + other_on * turns[axis]
+            near_inter[axis, 1] = spot_rim[1, axis] + other_on * turns[axis]
+            own_spot[axis] = near_plane[axis, 0, inner, :]
+            own_spot[2 + axis] = spot[0, axis, inner, :] + own_on * turns[axis][inner]
 
     def atom_heights(index):
         return (index >> 2).astype(jnp.float32) * 3.0 + pick(index & 3, atom_y)
@@ -306,19 +329,20 @@
         scaled = dist_sq * inverse_cut
         return fall * jnp.maximum(1.0 - scaled * scaled, 0.0)
 
-    for n, (col, step) in enumerate(PLANE):
-        dist_sq = parts(0, near_plane, col, step)
-        hop_plane[n] = envelope(dist_sq, lax.rsqrt(dist_sq)) * (v_pi * scale)
-    for n, (col, step) in enumerate(INTER):
-        dist_sq = parts(2, near_inter, col, step) + layer_gap * layer_gap
-        inverse = lax.rsqrt(dist_sq)
-        cosine_sq = (inverse * inverse) * (layer_gap * layer_gap)
-        mix = cosine_sq * ((sigma_part - v_pi) * scale) + v_pi * scale
-        hop_inter[n] = envelope(dist_sq, inverse) * mix
-
-    def unpack_ends(ends):
+    def find_hops():
+        for n, (col, step) in enumerate(PLANE):
+            dist_sq = parts(0, near_plane, col, step)
+            hop_plane[n] = envelope(dist_sq, lax.rsqrt(dist_sq)) * (v_pi * scale)
+        for n, (col, step) in enumerate(INTER):
+            dist_sq = parts(2, near_inter, col, step) + layer_gap * layer_gap
+            inverse = lax.rsqrt(dist_sq)
+            cosine_sq = (inverse * inverse) * (layer_gap * layer_gap)
+            mix = cosine_sq * ((sigma_part - v_pi) * scale) + v_pi * scale
+            hop_inter[n] = envelope(dist_sq, inverse) * mix
+
+    def unpack_ends(ends, columns):
         for layer in range(2):
-            for col in range(WIDE):
+            for col in columns:
                 side, own = rim_of(col)
                 for g in range(4):
                     low, high = ends[side, layer, 0, 0:8, :], ends[side, layer, 1, 0:8, :]
@@ -370,32 +394,55 @@
                     result[n, 0, x, y, 8 * g : 8 * g + 8, :] = value
 
     half = COLS // 2
-    unpack_ends(end_in)
-    for copy in right_rim + [right_tile]:
-        copy.wait_recv()
+    right_wide, left_wide = range(half, WIDE), range(half)
+
+    def arrive(copies):
+        for copy in copies:
+            copy.wait_recv()
+
+    arrive(near_right)
+    find_spots((1, 2))
+    find_hops()
+    unpack_ends(end_in, right_wide)
+    arrive(right_rim + [right_tile])
     apply(wide, prev_t, 0, wide2.at[0], RIM, half, half)
-    last = [send_side(wide2, layer, 1) for layer in (1, 0)]
-    last.append(send_tile(wide2, half, half))
-    for copy in left_rim + [left_tile]:
-        copy.wait_recv()
+    tile2 = [send_tile(wide2, half, half)]
+    from_left = [send_side(wide2, layer, 1) for layer in (1, 0)]
+    packed = pack_ends(wide2, end_out2.at[0], range(half, COLS))
+    from_left += [send_end(end_out2.at[0], end_in2, step) for step in CORNERS if step[1] > 0]
+    arrive(near_left)
+    find_spots((0, 1, 2))
+    find_hops()
+    unpack_ends(end_in, left_wide)
+    arrive(left_rim + [left_tile])
     apply(wide, prev_t, 0, wide2.at[0], RIM, 0, half)
-    pack_ends(wide2, end_out2)
-    last += [send_end(end_out2, end_in2, step) for step in ENDS + CORNERS]
-    last += [send_side(wide2, layer, -1) for layer in (1, 0)]
-    last.append(send_tile(wide2, 0, half))
+    tile2.append(send_tile(wide2, 0, half))
+    from_right = [send_side(wide2, layer, -1) for layer in (1, 0)]
+    pack_ends(wide2, end_out2.at[1], range(half), packed)
+    from_right += [
+        send_end(end_out2.at[1], end_in2, step) for step in ENDS + CORNERS if step[1] <= 0
+    ]
     to_blocks(wide2.at[0], RIM, 0)
-    for copy in last:
-        copy.wait_recv()
-    unpack_ends(end_in2)
-    apply(wide2, wide.at[0], RIM, second_t, 0, 0, COLS)
-    to_blocks(second_t, 0, 1)
     for copy in sent:
         copy.wait_send()
-
-
-def finish(result, first_ref, second_ref):
-    first_ref[...] = result[0]
-    second_ref[...] = result[1]
+    arrive(tile2 + from_right)
+    unpack_ends(end_in2, right_wide)
+    apply(wide2, wide.at[0], RIM, second_t, 0, half, half)
+    arrive(from_left)
+    unpack_ends(end_in2, left_wide)
+    apply(wide2, wide.at[0], RIM, second_t, 0, 0, half)
+    to_blocks(second_t, 0, 1)
+
+
+def finish(result, first_ref, second_ref, sem):
+    copies = [
+        pltpu.make_async_copy(result.at[n], target, sem.at[n])
+        for n, target in enumerate((first_ref, second_ref))
+    ]
+    for copy in copies:
+        copy.start()
+    for copy in copies:
+        copy.wait()
 
 
 def body(prev_vec, cur_vec, displace, potential):
@@ -404,7 +451,7 @@
     hbm, vmem = pl.BlockSpec(memory_space=pltpu.HBM), pl.BlockSpec(memory_space=pltpu.VMEM)
     result = pl.pallas_call(
         kernel,
-        out_shape=jax.ShapeDtypeStruct((2,) + cur_vec.shape, f32),
+        out_shape=pltpu.VMEM((2,) + cur_vec.shape, f32),
         in_specs=[hbm] * 4,
         out_specs=pl.BlockSpec(memory_space=pltpu.VMEM),
         scratch_shapes=[
@@ -417,9 +464,9 @@
             pltpu.VMEM((COLS, ROWS, 128), f32),
             pltpu.VMEM((2, WIDE, ROWS, 128), f32),
             pltpu.VMEM((2, WIDE, ROWS, 128), f32),
-            pltpu.VMEM((2, 24, 128), f32),
-            pltpu.VMEM((3, 2, 2, 24, 128), f32),
-            pltpu.VMEM((2, 8, 128), f32),
+            pltpu.VMEM((2, 16, 128), f32),
+            pltpu.VMEM((3, 2, 2, 16, 128), f32),
+            pltpu.VMEM((2, 2, 8, 128), f32),
             pltpu.VMEM((3, 2, 2, 8, 128), f32),
             pltpu.VMEM((3, 2, 2, COLS, 128), f32),
             pltpu.VMEM((2, WIDE, ROWS, 128), f32),
@@ -433,17 +480,23 @@
             pltpu.SemaphoreType.DMA((4,)),
             pltpu.SemaphoreType.DMA((MESSAGES,)),
             pltpu.SemaphoreType.DMA((MESSAGES,)),
+            pltpu.SemaphoreType.REGULAR((2,)),
+            pltpu.SemaphoreType.REGULAR,
         ],
         compiler_params=pltpu.CompilerParams(
             collective_id=0, has_side_effects=True, vmem_limit_bytes=VMEM_LIMIT
         ),
         name="two_terms",
-    )(prev_vec, cur_vec, displace, potential)
+    )(*[pltpu.with_memory_space_constraint(x, pltpu.HBM) for x in (prev_vec, cur_vec, displace, potential)])
     return pl.pallas_call(
         finish,
         out_shape=(jax.ShapeDtypeStruct(cur_vec.shape, f32),) * 2,
         in_specs=[vmem],
-        out_specs=(vmem, vmem),
+        out_specs=(hbm, hbm),
+        scratch_shapes=[
+            pltpu.SemaphoreType.DMA((2,)),
+        ],
+        compiler_params=pltpu.CompilerParams(vmem_limit_bytes=VMEM_LIMIT),
         name="finish",
     )(result)
 

time: 34.1 us -> 30.4 us (0.89)
  the two profiles are of different devices: /device:TPU:1 before, /device:TPU:16 now
where the time goes in v2:
time: 30.4 us; the launch traced here: 30.3 us
  Pallas kernels  29.7 us (98%)
  between operations  0.64 us (2%)
    pallas_call x1, Pallas kernels, body(): pl.pallas_call(kernel, out_shape=pltpu.VMEM((2,) + cur_vec.shape, f32), i...  28.9 us
    pallas_call x1, Pallas kernels, body(): pl.pallas_call(finish, out_shape=(jax.ShapeDtypeStruct(cur_vec.shape, f32...  0.72 us

profile of v2, /device:TPU:16, one launch (start us, length us, event | category | flops | bytes accessed | tf_op | source)
XLA Modules:
  0.0 30.3 jit_solution(13912546504298020326)
XLA Ops:
  0.6 28.9 %two_terms.1.result = f32[2,1,2,4,32,128]{5,4,3,2,1,0:T(8,128)S(1)} custom-call(f32[1,2,4,32,128]{4,3,2,1,0:T(8,128)} %prev_hbm.1, f32[1,2,4,32,128]{4,3,2,1,0:T(8,128)} %cur_hbm.1, f32[1,2,4,2,128]{4,3,2,1,0:T(2,128)} %disp_hbm.1, f32[1,2,4,128]{3,2,1,0:T(4,128)} %pot_hbm.1), custom_call_target="tpu_custom_call" | custom-call | tf_op jit(solution)/shard_map/two_terms/pallas_call | solution.py:452
  29.6 0.7 %finish.1 = (f32[1,2,4,32,128]{4,3,2,1,0:T(8,128)}, f32[1,2,4,32,128]{4,3,2,1,0:T(8,128)}) custom-call(f32[2,1,2,4,32,128]{5,4,3,2,1,0:T(8,128)S(1)} %two_terms.1.result), custom_call_target="tpu_custom_call" | custom-call | tf_op jit(solution)/shard_map/finish/pallas_call | solution.py:491

commit v3 on v2

--- a/solution.py
+++ b/solution.py
@@ -406,8 +406,8 @@
     unpack_ends(end_in, right_wide)
     arrive(right_rim + [right_tile])
     apply(wide, prev_t, 0, wide2.at[0], RIM, half, half)
+    from_left = [send_side(wide2, layer, 1) for layer in (1, 0)]
     tile2 = [send_tile(wide2, half, half)]
-    from_left = [send_side(wide2, layer, 1) for layer in (1, 0)]
     packed = pack_ends(wide2, end_out2.at[0], range(half, COLS))
     from_left += [send_end(end_out2.at[0], end_in2, step) for step in CORNERS if step[1] > 0]
     arrive(near_left)

time: 30.4 us -> 30.4 us (level)
  no operation moved by 1% of the time
where the time goes in v3:
time: 30.4 us; the launch traced here: 30.3 us
  Pallas kernels  29.7 us (98%)
  between operations  0.64 us (2%)
    pallas_call x1, Pallas kernels, body(): pl.pallas_call(kernel, out_shape=pltpu.VMEM((2,) + cur_vec.shape, f32), i...  28.9 us
    pallas_call x1, Pallas kernels, body(): pl.pallas_call(finish, out_shape=(jax.ShapeDtypeStruct(cur_vec.shape, f32...  0.72 us

profile of v3, /device:TPU:16, one launch (start us, length us, event | category | flops | bytes accessed | tf_op | source)
XLA Modules:
  0.0 30.3 jit_solution(14319696191845917878)
XLA Ops:
  0.6 28.9 %two_terms.1.result = f32[2,1,2,4,32,128]{5,4,3,2,1,0:T(8,128)S(1)} custom-call(f32[1,2,4,32,128]{4,3,2,1,0:T(8,128)} %prev_hbm.1, f32[1,2,4,32,128]{4,3,2,1,0:T(8,128)} %cur_hbm.1, f32[1,2,4,2,128]{4,3,2,1,0:T(2,128)} %disp_hbm.1, f32[1,2,4,128]{3,2,1,0:T(4,128)} %pot_hbm.1), custom_call_target="tpu_custom_call" | custom-call | tf_op jit(solution)/shard_map/two_terms/pallas_call | solution.py:452
  29.6 0.7 %finish.1 = (f32[1,2,4,32,128]{4,3,2,1,0:T(8,128)}, f32[1,2,4,32,128]{4,3,2,1,0:T(8,128)}) custom-call(f32[2,1,2,4,32,128]{5,4,3,2,1,0:T(8,128)S(1)} %two_terms.1.result), custom_call_target="tpu_custom_call" | custom-call | tf_op jit(solution)/shard_map/finish/pallas_call | solution.py:491
